TPU v7x, 256 devices: a whole 4x4x8 slice. The times are simulated.
256 devices in a mesh: gx: 16 (over y, x_hi, core), gy: 16 (over z, x_lo).
Axes of the slice: x: 4 (x_hi: 2, x_lo: 2; x = x_hi * 2 + x_lo), y: 4, z: 8, core: 2. Of those that a mesh axis runs over, the one named last changes fastest.
Arguments:
- tokens: bfloat16 [32, 32, 32, 768], P('gx', 'gy'), may hold values from -48 to 48
- w_qkv: bfloat16 [768, 2304], replicated, may hold values from -0.25 to 0.25
- w_out: bfloat16 [768, 768], replicated, may hold values from -0.21875 to 0.21875
- norm_gain: float32 [768], replicated, may hold values from 0.1 to 1.9
- norm_shift: float32 [768], replicated, may hold values from -3 to 3
- w_conv: bfloat16 [3, 3, 3, 768, 256], P(None, None, None, None, 'gx'), may hold values from -0.0390625 to 0.0390625
- conv_bias: float32 [256], replicated, may hold values from -0.5 to 0.5
Outputs:
- decoded: bfloat16 [32, 32, 32, 256], P('gx', 'gy')
All inputs are finite; a program needn't handle non-finite values.
Results may differ from a plain program's by a relative error of at most 0.015.
Values may be sent and summed in bfloat16 or wider, within the bound.
No kernel may reach another device: no remote copies, remote signals or barrier semaphores. Data moves between devices by JAX's collectives and lax.ppermute only.
A program may use at most 192 MiB of HBM per device.

v0:
```python
import math

import jax
import jax.numpy as jnp
from jax import lax
from jax.sharding import PartitionSpec as P

HEAD_DIM = 48


def padded_2(block, sides, width):
    for axis, dim in sides:
        count = lax.axis_size(axis)
        forward = [(i, i + 1) for i in range(count - 1)]
        forward.append((count - 1, 0))
        backward = [(target, source) for source, target in forward]
        low = lax.ppermute(
            lax.slice_in_dim(block, block.shape[dim] - width, None, axis=dim), axis, forward
        )
        high = lax.ppermute(lax.slice_in_dim(block, 0, width, axis=dim), axis, backward)
        block = jnp.concatenate([low, block, high], axis=dim)
    return block


def attend_block(carry, queries, key_block, value_block):
    running, totals, accum = carry
    scores = jnp.einsum(
        "qhd,khd->hqk", queries, key_block, preferred_element_type=jnp.float32
    ) / math.sqrt(HEAD_DIM)
    newest = jnp.maximum(running, jnp.max(scores, axis=-1))
    factor = jnp.exp(running - newest)
    expons = jnp.exp(scores - newest[..., None])
    totals = totals * factor + jnp.sum(expons, axis=-1)
    accum = accum * factor[..., None] + jnp.einsum(
        "hqk,khd->hqd", expons.astype(jnp.bfloat16), value_block, preferred_element_type=jnp.float32
    )
    return (newest, totals, accum)


def prepare(queries_grid):
    heads_here = queries_grid.shape[-1] // HEAD_DIM
    queries = queries_grid.reshape(-1, heads_here, HEAD_DIM)
    count_q = queries.shape[0]
    start_state = (
        jnp.full((heads_here, count_q), -1e30, jnp.float32),
        jnp.zeros((heads_here, count_q), jnp.float32),
        jnp.zeros((heads_here, count_q, HEAD_DIM), jnp.float32),
    )

    def fold_keys(carry, piece, start):
        keys_piece = piece[0].reshape(-1, heads_here, HEAD_DIM)
        values_piece = piece[1].reshape(-1, heads_here, HEAD_DIM)
        count_k = keys_piece.shape[0]
        block_rows = math.gcd(count_k, 2048)
        key_blocks = keys_piece.reshape(count_k // block_rows, block_rows, heads_here, HEAD_DIM)
        value_blocks = values_piece.reshape(count_k // block_rows, block_rows, heads_here, HEAD_DIM)

        def advance(state, pair):
            return (attend_block(state, queries, pair[0], pair[1]), None)

        carry, unused = lax.scan(advance, carry, (key_blocks, value_blocks))
        return carry

    return (start_state, fold_keys)


def finish(carry, grid_shape):
    result = carry[2] / carry[1][..., None]
    return result.transpose(1, 0, 2).reshape(grid_shape).astype(jnp.bfloat16)


def stencil(padded, kernel, offsets, out_x, out_y, out_z):
    width = padded.shape[3]
    columns = kernel.shape[4]
    total = jnp.zeros((out_x * out_y * out_z, columns), jnp.float32)
    for shift_x in range(3):
        for shift_y in range(3):
            for shift_z in range(3):
                window = padded[
                    shift_x : shift_x + out_x, shift_y : shift_y + out_y, shift_z : shift_z + out_z
                ].reshape(-1, width)
                total = total + jnp.dot(
                    window, kernel[shift_x, shift_y, shift_z], preferred_element_type=jnp.float32
                )
    return (total + offsets).astype(jnp.bfloat16).reshape(out_x, out_y, out_z, columns)


def shards(tokens, w_qkv, w_out, norm_gain, norm_shift, w_conv, conv_bias):
    size_x, size_y, size_z, width = tokens.shape
    rows = tokens.reshape(-1, width)
    packed = jnp.dot(rows, w_qkv, preferred_element_type=jnp.float32).astype(jnp.bfloat16)
    packed = packed.reshape(size_x, size_y, size_z, 3 * width)
    query_all = packed[..., :width]
    keys_all = packed[..., width : 2 * width]
    values_all = packed[..., 2 * width :]
    query_mine, keys_mine, values_mine = (
        lax.all_to_all(query_all, "gy", split_axis=3, concat_axis=1, tiled=True),
        lax.all_to_all(keys_all, "gy", split_axis=3, concat_axis=1, tiled=True),
        lax.all_to_all(values_all, "gy", split_axis=3, concat_axis=1, tiled=True),
    )
    start_state, fold_keys = prepare(query_mine)
    carry = fold_keys(
        start_state,
        (
            lax.all_gather(keys_mine, "gx", axis=0, tiled=True),
            lax.all_gather(values_mine, "gx", axis=0, tiled=True),
        ),
        jnp.int32(0),
    )
    attended = lax.all_to_all(
        finish(carry, query_mine.shape), "gy", split_axis=1, concat_axis=3, tiled=True
    )
    projected = jnp.dot(attended.reshape(-1, width), w_out, preferred_element_type=jnp.float32)
    center = jnp.mean(projected, axis=-1, keepdims=True)
    spread = jnp.mean((projected - center) ** 2, axis=-1, keepdims=True)
    normed = ((projected - center) / jnp.sqrt(spread + 1e-05) * norm_gain + norm_shift).astype(
        jnp.bfloat16
    )
    normed = normed.reshape(size_x, size_y, size_z, width)
    padded = padded_2(normed, (("gx", 0), ("gy", 1)), 1)
    padded = jnp.concatenate([padded[:, :, -1:], padded, padded[:, :, :1]], axis=2)
    return stencil(
        padded, lax.all_gather(w_conv, "gx", axis=4, tiled=True), conv_bias, size_x, size_y, size_z
    )


def solution(mesh):
    return jax.shard_map(
        shards,
        mesh=mesh,
        in_specs=(
            P("gx", "gy", None, None),
            P(),
            P(),
            P(),
            P(),
            P(None, None, None, None, "gx"),
            P(),
        ),
        out_specs=P("gx", "gy", None, None),
        check_vma=False,
    )
```

profile of v0, /device:TPU:32, one launch (start us, length us, event | category | flops | bytes accessed | tf_op | source)
XLA Modules:
  0.0 724.1 jit_solution(16310915899220504731)
XLA Ops:
  11.5 18.8 %all_to_all.66 = bf16[16,2,3072]{2,1,0:T(2,128)(2,1)S(1)} all-to-all(bf16[16,2,3072]{2,1,0:T(2,128)(2,1)S(1)} %reshape.181), channel_id=1, replica_groups=mesh['gx'=16,'gy'=16] {'gy'}, dimensions={0} | all-to-all | bytes 393216 | tf_op jit(solution)/shard_map/all_to_all | solution.py:98
  33.8 12.7 %all_to_all.67 = bf16[16,2,3072]{2,1,0:T(2,128)(2,1)S(1)} all-to-all(bf16[16,2,3072]{2,1,0:T(2,128)(2,1)S(1)} %reshape.185), channel_id=1, replica_groups=mesh['gx'=16,'gy'=16] {'gy'}, dimensions={0} | all-to-all | bytes 393216 | tf_op jit(solution)/shard_map/all_to_all | solution.py:99
  67.1 58.8 %all-gather.4.cloned.1.call-done = bf16[32,32,32,48]{2,1,0,3:T(8,128)(2,1)} async-done(((bf16[2,32,32,48]{2,1,0,3:T(8,128)(2,1)}), bf16[32,32,32,48]{2,1,0,3:T(8,128)(2,1)}) %all-gather.4.cloned.1.call-update) | async-done | bytes 3145744 | tf_op jit(solution)/shard_map/all_gather | solution.py:105
  125.9 16.2 %reshape_reshape.6 = bf16[16,2048,1,48]{1,0,3,2:T(8,128)(2,1)S(1)} reshape(bf16[32,32,32,48]{2,1,0,3:T(8,128)(2,1)} %all-gather.4.cloned.1.call-done) | data formatting | bytes 6291456 | tf_op jit(solution)/shard_map/reshape;reshape | solution.py:55
  145.5 76.8 %all-gather.6.cloned.1.call-done = bf16[32,32,32,48]{2,1,0,3:T(8,128)(2,1)} async-done(((bf16[2,32,32,48]{2,1,0,3:T(8,128)(2,1)}), bf16[32,32,32,48]{2,1,0,3:T(8,128)(2,1)}) %all-gather.6.cloned.1.call-update) | async-done | bytes 3145744 | tf_op jit(solution)/shard_map/all_gather | solution.py:106
  222.3 16.2 %reshape_reshape.7 = bf16[16,2048,1,48]{1,0,3,2:T(8,128)(2,1)S(1)} reshape(bf16[32,32,32,48]{2,1,0,3:T(8,128)(2,1)} %all-gather.6.cloned.1.call-done) | data formatting | bytes 6291456 | tf_op jit(solution)/shard_map/reshape;reshape | solution.py:56
  241.9 403.4 %while.15 = (s32[]{:T(128)}, f32[1,2048]{1,0:T(1,128)S(1)}, f32[1,2048]{1,0:T(1,128)S(1)}, f32[1,2048,48]{1,2,0:T(8,128)S(1)}, bf16[16,2048,1,48]{1,3,2,0:T(8,12...) while((s32[]{:T(128)}, f32[1,2048]{1,0:T(1,128)S(1)}, ...), condition=%wide.region_3.4_spmd.clone, body=%wide.region_0.3_spmd.clone.sunk | while | flops 839165952 | bytes 51840100 | solution.py:61
  241.9 9.2 %multiply_reduce_fusion.3 = (f32[2048]{0:T(1024)S(1)}, f32[2048,2048]{1,0:T(8,128)}) fusion(bf16[2048,1,48]{0,2,1:T(8,128)(2,1)} %get-tuple-element.222, bf16[16,2048,1,48]{1,3,2,0:T(8,128)(2,1)} %get-tuple-element.221, s32[]{:T(128)} %get-tuple-element.208), kind=kOutput, calls=%fused_computation.1.clone.1 | convolution fusion | flops 411039744 | bytes 17179136 | tf_op jit(solution)/shard_map/while/body/eval_jaxpr/qhd,khd->hqk/dot_general | solution.py:27
  251.2 8.6 %fusion.79 = f32[2048]{0:T(1024)S(1)} fusion(f32[2048,2048]{1,0:T(8,128)} %get-tuple-element.196, f32[2048]{0:T(1024)S(1)} %bitcast.224), kind=kLoop, calls=%fused_computation.3.clone.1 | loop fusion | flops 12580864 | bytes 16793600 | tf_op jit(solution)/shard_map/while/body/eval_jaxpr/reduce_sum | solution.py:33
  267.2 9.1 %multiply_reduce_fusion.3 = (f32[2048]{0:T(1024)S(1)}, f32[2048,2048]{1,0:T(8,128)}) fusion(bf16[2048,1,48]{0,2,1:T(8,128)(2,1)} %get-tuple-element.222, bf16[16,2048,1,48]{1,3,2,0:T(8,128)(2,1)} %get-tuple-element.221, s32[]{:T(128)} %get-tuple-element.208), kind=kOutput, calls=%fused_computation.1.clone.1 | convolution fusion | flops 411039744 | bytes 17179136 | tf_op jit(solution)/shard_map/while/body/eval_jaxpr/qhd,khd->hqk/dot_general | solution.py:27
  276.4 8.7 %fusion.79 = f32[2048]{0:T(1024)S(1)} fusion(f32[2048,2048]{1,0:T(8,128)} %get-tuple-element.196, f32[2048]{0:T(1024)S(1)} %bitcast.224), kind=kLoop, calls=%fused_computation.3.clone.1 | loop fusion | flops 12580864 | bytes 16793600 | tf_op jit(solution)/shard_map/while/body/eval_jaxpr/reduce_sum | solution.py:33
  292.5 9.4 %multiply_reduce_fusion.3 = (f32[2048]{0:T(1024)S(1)}, f32[2048,2048]{1,0:T(8,128)}) fusion(bf16[2048,1,48]{0,2,1:T(8,128)(2,1)} %get-tuple-element.222, bf16[16,2048,1,48]{1,3,2,0:T(8,128)(2,1)} %get-tuple-element.221, s32[]{:T(128)} %get-tuple-element.208), kind=kOutput, calls=%fused_computation.1.clone.1 | convolution fusion | flops 411039744 | bytes 17179136 | tf_op jit(solution)/shard_map/while/body/eval_jaxpr/qhd,khd->hqk/dot_general | solution.py:27
  301.9 8.9 %fusion.79 = f32[2048]{0:T(1024)S(1)} fusion(f32[2048,2048]{1,0:T(8,128)} %get-tuple-element.196, f32[2048]{0:T(1024)S(1)} %bitcast.224), kind=kLoop, calls=%fused_computation.3.clone.1 | loop fusion | flops 12580864 | bytes 16793600 | tf_op jit(solution)/shard_map/while/body/eval_jaxpr/reduce_sum | solution.py:33
  318.2 9.1 %multiply_reduce_fusion.3 = (f32[2048]{0:T(1024)S(1)}, f32[2048,2048]{1,0:T(8,128)}) fusion(bf16[2048,1,48]{0,2,1:T(8,128)(2,1)} %get-tuple-element.222, bf16[16,2048,1,48]{1,3,2,0:T(8,128)(2,1)} %get-tuple-element.221, s32[]{:T(128)} %get-tuple-element.208), kind=kOutput, calls=%fused_computation.1.clone.1 | convolution fusion | flops 411039744 | bytes 17179136 | tf_op jit(solution)/shard_map/while/body/eval_jaxpr/qhd,khd->hqk/dot_general | solution.py:27
  327.3 8.5 %fusion.79 = f32[2048]{0:T(1024)S(1)} fusion(f32[2048,2048]{1,0:T(8,128)} %get-tuple-element.196, f32[2048]{0:T(1024)S(1)} %bitcast.224), kind=kLoop, calls=%fused_computation.3.clone.1 | loop fusion | flops 12580864 | bytes 16793600 | tf_op jit(solution)/shard_map/while/body/eval_jaxpr/reduce_sum | solution.py:33
  343.4 9.1 %multiply_reduce_fusion.3 = (f32[2048]{0:T(1024)S(1)}, f32[2048,2048]{1,0:T(8,128)}) fusion(bf16[2048,1,48]{0,2,1:T(8,128)(2,1)} %get-tuple-element.222, bf16[16,2048,1,48]{1,3,2,0:T(8,128)(2,1)} %get-tuple-element.221, s32[]{:T(128)} %get-tuple-element.208), kind=kOutput, calls=%fused_computation.1.clone.1 | convolution fusion | flops 411039744 | bytes 17179136 | tf_op jit(solution)/shard_map/while/body/eval_jaxpr/qhd,khd->hqk/dot_general | solution.py:27
  352.5 8.5 %fusion.79 = f32[2048]{0:T(1024)S(1)} fusion(f32[2048,2048]{1,0:T(8,128)} %get-tuple-element.196, f32[2048]{0:T(1024)S(1)} %bitcast.224), kind=kLoop, calls=%fused_computation.3.clone.1 | loop fusion | flops 12580864 | bytes 16793600 | tf_op jit(solution)/shard_map/while/body/eval_jaxpr/reduce_sum | solution.py:33
  368.5 9.1 %multiply_reduce_fusion.3 = (f32[2048]{0:T(1024)S(1)}, f32[2048,2048]{1,0:T(8,128)}) fusion(bf16[2048,1,48]{0,2,1:T(8,128)(2,1)} %get-tuple-element.222, bf16[16,2048,1,48]{1,3,2,0:T(8,128)(2,1)} %get-tuple-element.221, s32[]{:T(128)} %get-tuple-element.208), kind=kOutput, calls=%fused_computation.1.clone.1 | convolution fusion | flops 411039744 | bytes 17179136 | tf_op jit(solution)/shard_map/while/body/eval_jaxpr/qhd,khd->hqk/dot_general | solution.py:27
  377.7 8.5 %fusion.79 = f32[2048]{0:T(1024)S(1)} fusion(f32[2048,2048]{1,0:T(8,128)} %get-tuple-element.196, f32[2048]{0:T(1024)S(1)} %bitcast.224), kind=kLoop, calls=%fused_computation.3.clone.1 | loop fusion | flops 12580864 | bytes 16793600 | tf_op jit(solution)/shard_map/while/body/eval_jaxpr/reduce_sum | solution.py:33
  393.7 9.1 %multiply_reduce_fusion.3 = (f32[2048]{0:T(1024)S(1)}, f32[2048,2048]{1,0:T(8,128)}) fusion(bf16[2048,1,48]{0,2,1:T(8,128)(2,1)} %get-tuple-element.222, bf16[16,2048,1,48]{1,3,2,0:T(8,128)(2,1)} %get-tuple-element.221, s32[]{:T(128)} %get-tuple-element.208), kind=kOutput, calls=%fused_computation.1.clone.1 | convolution fusion | flops 411039744 | bytes 17179136 | tf_op jit(solution)/shard_map/while/body/eval_jaxpr/qhd,khd->hqk/dot_general | solution.py:27
  418.8 9.1 %multiply_reduce_fusion.3 = (f32[2048]{0:T(1024)S(1)}, f32[2048,2048]{1,0:T(8,128)}) fusion(bf16[2048,1,48]{0,2,1:T(8,128)(2,1)} %get-tuple-element.222, bf16[16,2048,1,48]{1,3,2,0:T(8,128)(2,1)} %get-tuple-element.221, s32[]{:T(128)} %get-tuple-element.208), kind=kOutput, calls=%fused_computation.1.clone.1 | convolution fusion | flops 411039744 | bytes 17179136 | tf_op jit(solution)/shard_map/while/body/eval_jaxpr/qhd,khd->hqk/dot_general | solution.py:27
  444.0 9.1 %multiply_reduce_fusion.3 = (f32[2048]{0:T(1024)S(1)}, f32[2048,2048]{1,0:T(8,128)}) fusion(bf16[2048,1,48]{0,2,1:T(8,128)(2,1)} %get-tuple-element.222, bf16[16,2048,1,48]{1,3,2,0:T(8,128)(2,1)} %get-tuple-element.221, s32[]{:T(128)} %get-tuple-element.208), kind=kOutput, calls=%fused_computation.1.clone.1 | convolution fusion | flops 411039744 | bytes 17179136 | tf_op jit(solution)/shard_map/while/body/eval_jaxpr/qhd,khd->hqk/dot_general | solution.py:27
  469.2 9.1 %multiply_reduce_fusion.3 = (f32[2048]{0:T(1024)S(1)}, f32[2048,2048]{1,0:T(8,128)}) fusion(bf16[2048,1,48]{0,2,1:T(8,128)(2,1)} %get-tuple-element.222, bf16[16,2048,1,48]{1,3,2,0:T(8,128)(2,1)} %get-tuple-element.221, s32[]{:T(128)} %get-tuple-element.208), kind=kOutput, calls=%fused_computation.1.clone.1 | convolution fusion | flops 411039744 | bytes 17179136 | tf_op jit(solution)/shard_map/while/body/eval_jaxpr/qhd,khd->hqk/dot_general | solution.py:27
  494.3 9.1 %multiply_reduce_fusion.3 = (f32[2048]{0:T(1024)S(1)}, f32[2048,2048]{1,0:T(8,128)}) fusion(bf16[2048,1,48]{0,2,1:T(8,128)(2,1)} %get-tuple-element.222, bf16[16,2048,1,48]{1,3,2,0:T(8,128)(2,1)} %get-tuple-element.221, s32[]{:T(128)} %get-tuple-element.208), kind=kOutput, calls=%fused_computation.1.clone.1 | convolution fusion | flops 411039744 | bytes 17179136 | tf_op jit(solution)/shard_map/while/body/eval_jaxpr/qhd,khd->hqk/dot_general | solution.py:27
  519.5 9.1 %multiply_reduce_fusion.3 = (f32[2048]{0:T(1024)S(1)}, f32[2048,2048]{1,0:T(8,128)}) fusion(bf16[2048,1,48]{0,2,1:T(8,128)(2,1)} %get-tuple-element.222, bf16[16,2048,1,48]{1,3,2,0:T(8,128)(2,1)} %get-tuple-element.221, s32[]{:T(128)} %get-tuple-element.208), kind=kOutput, calls=%fused_computation.1.clone.1 | convolution fusion | flops 411039744 | bytes 17179136 | tf_op jit(solution)/shard_map/while/body/eval_jaxpr/qhd,khd->hqk/dot_general | solution.py:27
  528.6 8.5 %fusion.79 = f32[2048]{0:T(1024)S(1)} fusion(f32[2048,2048]{1,0:T(8,128)} %get-tuple-element.196, f32[2048]{0:T(1024)S(1)} %bitcast.224), kind=kLoop, calls=%fused_computation.3.clone.1 | loop fusion | flops 12580864 | bytes 16793600 | tf_op jit(solution)/shard_map/while/body/eval_jaxpr/reduce_sum | solution.py:33
  544.7 9.1 %multiply_reduce_fusion.3 = (f32[2048]{0:T(1024)S(1)}, f32[2048,2048]{1,0:T(8,128)}) fusion(bf16[2048,1,48]{0,2,1:T(8,128)(2,1)} %get-tuple-element.222, bf16[16,2048,1,48]{1,3,2,0:T(8,128)(2,1)} %get-tuple-element.221, s32[]{:T(128)} %get-tuple-element.208), kind=kOutput, calls=%fused_computation.1.clone.1 | convolution fusion | flops 411039744 | bytes 17179136 | tf_op jit(solution)/shard_map/while/body/eval_jaxpr/qhd,khd->hqk/dot_general | solution.py:27
  569.8 9.1 %multiply_reduce_fusion.3 = (f32[2048]{0:T(1024)S(1)}, f32[2048,2048]{1,0:T(8,128)}) fusion(bf16[2048,1,48]{0,2,1:T(8,128)(2,1)} %get-tuple-element.222, bf16[16,2048,1,48]{1,3,2,0:T(8,128)(2,1)} %get-tuple-element.221, s32[]{:T(128)} %get-tuple-element.208), kind=kOutput, calls=%fused_computation.1.clone.1 | convolution fusion | flops 411039744 | bytes 17179136 | tf_op jit(solution)/shard_map/while/body/eval_jaxpr/qhd,khd->hqk/dot_general | solution.py:27
  595.0 9.1 %multiply_reduce_fusion.3 = (f32[2048]{0:T(1024)S(1)}, f32[2048,2048]{1,0:T(8,128)}) fusion(bf16[2048,1,48]{0,2,1:T(8,128)(2,1)} %get-tuple-element.222, bf16[16,2048,1,48]{1,3,2,0:T(8,128)(2,1)} %get-tuple-element.221, s32[]{:T(128)} %get-tuple-element.208), kind=kOutput, calls=%fused_computation.1.clone.1 | convolution fusion | flops 411039744 | bytes 17179136 | tf_op jit(solution)/shard_map/while/body/eval_jaxpr/qhd,khd->hqk/dot_general | solution.py:27
  620.1 9.1 %multiply_reduce_fusion.3 = (f32[2048]{0:T(1024)S(1)}, f32[2048,2048]{1,0:T(8,128)}) fusion(bf16[2048,1,48]{0,2,1:T(8,128)(2,1)} %get-tuple-element.222, bf16[16,2048,1,48]{1,3,2,0:T(8,128)(2,1)} %get-tuple-element.221, s32[]{:T(128)} %get-tuple-element.208), kind=kOutput, calls=%fused_computation.1.clone.1 | convolution fusion | flops 411039744 | bytes 17179136 | tf_op jit(solution)/shard_map/while/body/eval_jaxpr/qhd,khd->hqk/dot_general | solution.py:27
  629.3 8.5 %fusion.79 = f32[2048]{0:T(1024)S(1)} fusion(f32[2048,2048]{1,0:T(8,128)} %get-tuple-element.196, f32[2048]{0:T(1024)S(1)} %bitcast.224), kind=kLoop, calls=%fused_computation.3.clone.1 | loop fusion | flops 12580864 | bytes 16793600 | tf_op jit(solution)/shard_map/while/body/eval_jaxpr/reduce_sum | solution.py:33
  647.7 17.2 %all_to_all.68 = bf16[16,2,3072]{2,1,0:T(2,128)(2,1)S(1)} all-to-all(bf16[16,2,3072]{2,1,0:T(2,128)(2,1)S(1)} %reshape.187), channel_id=1, replica_groups=mesh['gx'=16,'gy'=16] {'gy'}, dimensions={0} | all-to-all | bytes 393216 | tf_op jit(solution)/shard_map/all_to_all | solution.py:110
  (196 shorter events, 277.8 us)
Async XLA Ops:
  6.5 2.0 copy-start
  6.5 119.3 %all-gather.4.cloned.1.call-start = ((), (), s32[]{:S(2)}) async-start(), calls=%async_computation.4 | async-start | bytes 13369344 | tf_op jit(solution)/shard_map/all_gather | solution.py:105
  32.5 189.8 %all-gather.6.cloned.1.call-start = ((), (), s32[]{:S(2)}) async-start(), calls=%async_computation.5 | async-start | bytes 13369344 | tf_op jit(solution)/shard_map/all_gather | solution.py:106
  50.7 13.8 %all-to-all-start.1 = ((bf16[16,2,3072]{2,1,0:T(2,128)(2,1)}), bf16[16,2,3072]{2,1,0:T(2,128)(2,1)S(1)}, u32[]{:S(2)}, u32[]{:S(2)}) async-start(bf16[16,2,3072]{2,1,0:T(2,128)(2,1)} %reshape.183), calls=%async_computation.1 | async-start | bytes 393216 | tf_op jit(solution)/shard_map/all_to_all | solution.py:97
  55.8 635.0 %all-gather.8.cloned.1.call-start = ((), (), s32[]{:S(2)}) async-start(), calls=%async_computation.6 | async-start | bytes 11280384 | tf_op jit(solution)/shard_map/all_gather | solution.py:123
  241.9 424.3 %copy-start.5 = (bf16[768,768]{1,0:T(8,128)(2,1)S(1)}, bf16[768,768]{1,0:T(8,128)(2,1)}, u32[]{:S(2)}) copy-start(bf16[768,768]{1,0:T(8,128)(2,1)} %param.11) | copy-start | bytes 3538948
  241.9 424.9 %copy-start.16 = (f32[768]{0:T(1024)S(1)}, f32[768]{0:T(1024)}, u32[]{:S(2)}) copy-start(f32[768]{0:T(1024)} %param.13) | copy-start | bytes 9220
  241.9 424.9 %copy-start.17 = (f32[768]{0:T(1024)S(1)}, f32[768]{0:T(1024)}, u32[]{:S(2)}) copy-start(f32[768]{0:T(1024)} %param.12) | copy-start | bytes 9220
  667.0 20.1 %copy-start.2 = (bf16[128,768]{1,0:T(8,128)(2,1)}, bf16[128,768]{1,0:T(8,128)(2,1)S(1)}, u32[]{:S(2)}) copy-start(bf16[128,768]{1,0:T(8,128)(2,1)S(1)} %add_convert_fusion) | copy-start | bytes 589828
  667.0 8.2 %collective-permute-start = (bf16[1,2,32,768]{3,2,1,0:T(8,128)(2,1)S(1)}, bf16[1,2,32,768]{3,2,1,0:T(8,128)(2,1)S(1)}, u32[]{:S(2)}, u32[]{:S(2)}) collective-permute-start(bf16[1,2,32,768]{3,2,1,0:T(8,128)(2,1)S(1)} %bitcast.271), channel_id=1, source_target_pairs={{0,16},{16,32},{32,48},{48,64},{64,80},{80,96},{96,112},{112,128},... | collective-permute-start | bytes 294920 | tf_op jit(solution)/shard_map/ppermute | solution.py:17
  667.1 8.1 %collective-permute-start.1 = (bf16[1,2,32,768]{3,2,1,0:T(8,128)(2,1)S(1)}, bf16[1,2,32,768]{3,2,1,0:T(8,128)(2,1)S(1)}, u32[]{:S(2)}, u32[]{:S(2)}) collective-permute-start(bf16[1,2,32,768]{3,2,1,0:T(8,128)(2,1)S(1)} %bitcast.270), channel_id=1, source_target_pairs={{16,0},{32,16},{48,32},{64,48},{80,64},{96,80},{112,96},{128,112},... | collective-permute-start | bytes 294920 | tf_op jit(solution)/shard_map/ppermute | solution.py:20
  675.3 9.0 %collective-permute-start.2 = (bf16[4,1,32,768]{3,2,1,0:T(8,128)(2,1)S(1)}, bf16[4,1,32,768]{3,2,1,0:T(8,128)(2,1)S(1)}, u32[]{:S(2)}, u32[]{:S(2)}) collective-permute-start(bf16[4,1,32,768]{3,2,1,0:T(8,128)(2,1)S(1)} %get-tuple-element.137), channel_id=1, source_target_pairs={{0,1},{1,2},{2,3},{3,4},{4,5},{5,6},{6,7},{7,8},{8,9},{9,10},{10,1... | collective-permute-start | bytes 589832 | tf_op jit(solution)/shard_map/ppermute | solution.py:17
  676.5 10.2 %collective-permute-start.3 = (bf16[4,1,32,768]{3,2,1,0:T(8,128)(2,1)S(1)}, bf16[4,1,32,768]{3,2,1,0:T(8,128)(2,1)S(1)}, u32[]{:S(2)}, u32[]{:S(2)}) collective-permute-start(bf16[4,1,32,768]{3,2,1,0:T(8,128)(2,1)S(1)} %get-tuple-element.138), channel_id=1, source_target_pairs={{1,0},{2,1},{3,2},{4,3},{5,4},{6,5},{7,6},{8,7},{9,8},{10,9},{11,1... | collective-permute-start | bytes 589832 | tf_op jit(solution)/shard_map/ppermute | solution.py:20
  690.8 19.2 %copy-start.3 = (bf16[128,768]{1,0:T(8,128)(2,1)S(1)}, bf16[128,768]{1,0:T(8,128)(2,1)}, u32[]{:S(2)}) copy-start(bf16[128,768]{1,0:T(8,128)(2,1)} %copy-done.2) | copy-start | bytes 589828
  690.8 19.2 %copy-start.4 = (bf16[3,3,3,768,256]{3,4,2,1,0:T(8,128)(2,1)S(1)}, bf16[3,3,3,768,256]{3,4,2,1,0:T(8,128)(2,1)}, u32[]{:S(2)}) copy-start(bf16[3,3,3,768,256]{3,4,2,1,0:T(8,128)(2,1)} %all-gather.8.cloned.1.call-done) | copy-start | bytes 31850500
  690.8 19.5 %copy-start.7 = (bf16[2,2,32,768]{3,2,1,0:T(8,128)(2,1)S(1)}, bf16[2,2,32,768]{3,2,1,0:T(8,128)(2,1)}, u32[]{:S(2)}) copy-start(bf16[2,2,32,768]{3,2,1,0:T(8,128)(2,1)} %get-tuple-element.109) | copy-start | bytes 589828
  690.8 21.0 %copy-start.14 = (bf16[2,2,32,768]{3,2,1,0:T(8,128)(2,1)S(1)}, bf16[2,2,32,768]{3,2,1,0:T(8,128)(2,1)}, u32[]{:S(2)}) copy-start(bf16[2,2,32,768]{3,2,1,0:T(8,128)(2,1)} %get-tuple-element.120) | copy-start | bytes 589828
  690.8 21.3 %copy-start.11 = (bf16[2,2,32,768]{3,2,1,0:T(8,128)(2,1)S(1)}, bf16[2,2,32,768]{3,2,1,0:T(8,128)(2,1)}, u32[]{:S(2)}) copy-start(bf16[2,2,32,768]{3,2,1,0:T(8,128)(2,1)} %get-tuple-element.127) | copy-start | bytes 589828
  690.8 21.6 %copy-start.15 = (bf16[2,2,32,768]{3,2,1,0:T(8,128)(2,1)S(1)}, bf16[2,2,32,768]{3,2,1,0:T(8,128)(2,1)}, u32[]{:S(2)}) copy-start(bf16[2,2,32,768]{3,2,1,0:T(8,128)(2,1)} %get-tuple-element.111) | copy-start | bytes 589828
  690.8 21.9 %copy-start.12 = (bf16[2,2,32,768]{3,2,1,0:T(8,128)(2,1)S(1)}, bf16[2,2,32,768]{3,2,1,0:T(8,128)(2,1)}, u32[]{:S(2)}) copy-start(bf16[2,2,32,768]{3,2,1,0:T(8,128)(2,1)} %get-tuple-element.119) | copy-start | bytes 589828
  690.9 23.4 %copy-start.13 = (bf16[2,2,32,768]{3,2,1,0:T(8,128)(2,1)S(1)}, bf16[2,2,32,768]{3,2,1,0:T(8,128)(2,1)}, u32[]{:S(2)}) copy-start(bf16[2,2,32,768]{3,2,1,0:T(8,128)(2,1)} %get-tuple-element.110) | copy-start | bytes 589828
  690.9 23.7 %copy-start.10 = (bf16[2,2,32,768]{3,2,1,0:T(8,128)(2,1)S(1)}, bf16[2,2,32,768]{3,2,1,0:T(8,128)(2,1)}, u32[]{:S(2)}) copy-start(bf16[2,2,32,768]{3,2,1,0:T(8,128)(2,1)} %get-tuple-element.118) | copy-start | bytes 589828
  690.9 25.2 %copy-start.9 = (bf16[2,2,32,768]{3,2,1,0:T(8,128)(2,1)S(1)}, bf16[2,2,32,768]{3,2,1,0:T(8,128)(2,1)}, u32[]{:S(2)}) copy-start(bf16[2,2,32,768]{3,2,1,0:T(8,128)(2,1)} %get-tuple-element.117) | copy-start | bytes 589828
  690.9 25.4 %copy-start.8 = (bf16[2,2,32,768]{3,2,1,0:T(8,128)(2,1)S(1)}, bf16[2,2,32,768]{3,2,1,0:T(8,128)(2,1)}, u32[]{:S(2)}) copy-start(bf16[2,2,32,768]{3,2,1,0:T(8,128)(2,1)} %get-tuple-element.126) | copy-start | bytes 589828
  692.3 24.3 %copy-start.6 = (bf16[2,2,32,768]{3,2,1,0:T(8,128)(2,1)S(1)}, bf16[2,2,32,768]{3,2,1,0:T(8,128)(2,1)}, u32[]{:S(2)}) copy-start(bf16[2,2,32,768]{3,2,1,0:T(8,128)(2,1)} %get-tuple-element.108) | copy-start | bytes 589828
  692.3 24.3 %copy-start.18 = (f32[256]{0:T(256)S(1)}, f32[256]{0:T(256)}, u32[]{:S(2)}) copy-start(f32[256]{0:T(256)} %param.15) | copy-start | bytes 3076
  694.3 23.3 %copy-start.1 = (bf16[768,2304]{1,0:T(8,128)(2,1)S(1)}, bf16[768,2304]{1,0:T(8,128)(2,1)}, u32[]{:S(2)}) copy-start(bf16[768,2304]{1,0:T(8,128)(2,1)} %param.10) | copy-start | bytes 10616836
Sparse Core Ops, SparseCore 0:
  32.6 93.2 all-gather.3
  128.6 93.5 all-gather.5
  225.1 85.2 all-gather.7
where the time goes:
time: 726 us; the launch traced here: 724 us
  matrix products  293 us (40%)
  waiting for transfers between devices  154 us (21%)
  other arithmetic  140 us (19%)
  local copies, waits for them, and re-layouts  60.1 us (8%)
  blocking collectives  48.7 us (7%)
  starting transfers between devices  13.7 us (2%)
  between operations  13.6 us (2%)
    dot_general x16, matrix products, attend_block(): jnp.einsum('qhd,khd->hqk', queries, key_block, preferred_element_type=jnp...  147 us
    reduce_sum x16, other arithmetic, attend_block(): totals = totals * factor + jnp.sum(expons, axis=-1)  137 us
    dot_general x16, matrix products, attend_block(): jnp.einsum('hqk,khd->hqd', expons.astype(jnp.bfloat16), value_block, pref...  118 us
    all_gather x1, waiting for transfers between devices, shards(): lax.all_gather(values_mine, 'gx', axis=0, tiled=True)  76.8 us
    all_gather x1, waiting for transfers between devices, shards(): lax.all_gather(keys_mine, 'gx', axis=0, tiled=True)  58.8 us
    dot_general x27, matrix products, stencil(): jnp.dot(window, kernel[shift_x, shift_y, shift_z], preferred_element_type...  26.5 us
    all_to_all x1, blocking collectives, shards(): lax.all_to_all(keys_all, 'gy', split_axis=3, concat_axis=1, tiled=True)  18.8 us
    all_to_all x1, blocking collectives, shards(): lax.all_to_all(finish(carry, query_mine.shape), 'gy', split_axis=1, conca...  17.2 us
  transfers between devices with their start and end apart: 8, of which 6 were waited for; matrix products, arithmetic and copies ran while one was open for 63% of the time, Pallas kernels for 0%

commit v1 on v0

v1 whole, which is shorter than its diff:
```python
import functools
import math

import jax
import jax.numpy as jnp
from jax import lax
from jax.experimental import pallas as pl
from jax.experimental.pallas import tpu as pltpu
from jax.sharding import PartitionSpec as P

HEADS = 16
HD = 48
D = 768
COUT = 256
SRC = 16
T = 128
NQ = SRC * T
CK = SRC * T
Q2 = 2 * NQ
QT = 1024
KROWS = 128
ORS = 64
SHIFT_ROW = 2 * HD
SUM_ROW = HD
SCALE = math.log2(math.e) / math.sqrt(HD)
SAFE_SUM = 2.0**100
VMEM = pl.BlockSpec(memory_space=pltpu.VMEM)
ANY = pl.BlockSpec(memory_space=pl.ANY)
BF = jnp.bfloat16
F32 = jnp.float32


def _params(mb=48):
    return pltpu.CompilerParams(vmem_limit_bytes=mb * 2**20)


def _cost(flops, nbytes, trans=0):
    return pl.CostEstimate(flops=int(flops), bytes_accessed=int(nbytes), transcendentals=int(trans))


def _qkv_kernel(x_ref, w_ref, o_ref):
    x = x_ref[...]
    for part in range(3):
        cols = pl.ds(part * D, D)
        y = jnp.dot(x, w_ref[:, cols], preferred_element_type=F32)
        yt = y.T.astype(BF)
        for h in range(HEADS):
            o_ref[h, part * HD : (part + 1) * HD, :] = yt[h * HD : (h + 1) * HD, :]


def _qkv(x, w):
    return pl.pallas_call(
        _qkv_kernel,
        out_shape=jax.ShapeDtypeStruct((HEADS, 3 * HD, T), BF),
        in_specs=[VMEM, VMEM],
        out_specs=VMEM,
        compiler_params=_params(),
        cost_estimate=_cost(2 * T * D * 3 * D, 5e6),
        name="qkv_projection",
    )(x, w)


def _fill_chunk(kv_ref, kp_ref, vp_ref, base):
    row = lax.broadcasted_iota(jnp.int32, (KROWS - 2 * HD, T), 0)
    shift_on = jnp.where(row < 3, 1.0, 0.0).astype(BF)
    vrow = lax.broadcasted_iota(jnp.int32, (ORS - HD, T), 0)
    ones = jnp.where(vrow == 0, 1.0, 0.0).astype(BF)
    for s in range(SRC):
        kt = kv_ref[s, 0:HD, :]
        block = jnp.concatenate([kt, kt, shift_on], axis=0)
        at = base + s * T
        kp_ref[at : at + T, :] = block.T
        vp_ref[0:HD, at : at + T] = kv_ref[s, HD : 2 * HD, :]
        vp_ref[HD:ORS, at : at + T] = ones


def _set_shift(qa_ref, cols, m):
    hi = m.astype(BF)
    rest = m - hi.astype(F32)
    mid = rest.astype(BF)
    low = (rest - mid.astype(F32)).astype(BF)
    row = lax.broadcasted_iota(jnp.int32, (16, m.shape[1]), 0)
    rows = jnp.where(
        row == 0, hi.astype(F32), jnp.where(row == 1, mid.astype(F32), jnp.where(row == 2, low.astype(F32), 0.0))
    )
    qa_ref[SHIFT_ROW : SHIFT_ROW + 16, cols] = (-rows).astype(BF)


def _tile(i):
    return pl.ds(pl.multiple_of(i * QT, QT), QT)


def _accumulate(qa_ref, kp_ref, vp_ref, acc_in, acc_out, chunks):
    def body(i, carry):
        cols = _tile(i)
        q = qa_ref[:, cols]
        acc = acc_in[:, cols] if acc_in is not None else jnp.zeros((ORS, QT), F32)
        for c in range(chunks):
            s = jnp.dot(kp_ref[c * CK : (c + 1) * CK, :], q, preferred_element_type=F32)
            p = jnp.exp2(s).astype(BF)
            acc = acc + jnp.dot(vp_ref[:, c * CK : (c + 1) * CK], p, preferred_element_type=F32)
        acc_out[:, cols] = acc
        return carry

    lax.fori_loop(0, Q2 // QT, body, 0)


def _first_kernel(q_own, q_sib, kv_ref, qa_ref, m_ref, acc_ref, kp_ref, vp_ref):
    _fill_chunk(kv_ref, kp_ref, vp_ref, 0)
    for part, q_ref in enumerate((q_own, q_sib)):
        for s in range(SRC):
            cols = pl.ds(part * NQ + s * T, T)
            q = q_ref[s, 0:HD, :].astype(F32) * SCALE
            hi = q.astype(BF)
            qa_ref[0:HD, cols] = hi
            qa_ref[HD : 2 * HD, cols] = (q - hi.astype(F32)).astype(BF)
    qa_ref[SHIFT_ROW:KROWS, :] = jnp.zeros((KROWS - SHIFT_ROW, Q2), BF)

    def start(i, carry):
        cols = _tile(i)
        s = jnp.dot(kp_ref[0:256, :], qa_ref[:, cols], preferred_element_type=F32)
        m = jnp.max(s, axis=0, keepdims=True)
        m_ref[:, cols] = jnp.broadcast_to(m, (8, QT))
        _set_shift(qa_ref, cols, m)
        return carry

    lax.fori_loop(0, Q2 // QT, start, 0)
    _accumulate(qa_ref, kp_ref, vp_ref, None, acc_ref, 1)


def _next_kernel(chunks, qa_ref, acc_in, *refs):
    kvs, (acc_out, kp_ref, vp_ref) = refs[:chunks], refs[chunks:]
    for c in range(chunks):
        _fill_chunk(kvs[c], kp_ref, vp_ref, c * CK)
    _accumulate(qa_ref, kp_ref, vp_ref, acc_in, acc_out, chunks)


def _redo(qa_ref, m_ref, acc_ref, kp_ref, vp_ref, kvs, buf, sem):
    def load(c):
        for n, ref in enumerate(kvs):

            @pl.when(c == n)
            def _():
                copy = pltpu.make_async_copy(ref, buf, sem)
                copy.start()
                copy.wait()

        _fill_chunk(buf, kp_ref, vp_ref, 0)

    qa_ref[SHIFT_ROW:KROWS, :] = jnp.zeros((KROWS - SHIFT_ROW, Q2), BF)

    def find(c, carry):
        load(c)

        def body(i, inner):
            cols = _tile(i)
            s = jnp.dot(kp_ref[0:CK, :], qa_ref[:, cols], preferred_element_type=F32)
            m_ref[:, cols] = jnp.maximum(m_ref[:, cols], jnp.max(s, axis=0, keepdims=True))
            return inner

        return lax.fori_loop(0, Q2 // QT, body, carry)

    lax.fori_loop(0, len(kvs), find, 0)

    def shift(i, carry):
        cols = _tile(i)
        _set_shift(qa_ref, cols, m_ref[0:1, cols])
        acc_ref[:, cols] = jnp.zeros((ORS, QT), F32)
        return carry

    lax.fori_loop(0, Q2 // QT, shift, 0)

    def add(c, carry):
        load(c)
        _accumulate(qa_ref, kp_ref, vp_ref, acc_ref, acc_ref, 1)
        return carry

    lax.fori_loop(0, len(kvs), add, 0)


def _last_kernel(qa_in, m_in, acc_in, kv_a, kv_b, *refs):
    kvs, (own_ref, sib_ref, qa_ref, m_ref, acc_ref, kp_ref, vp_ref, buf, sem) = refs[:8], refs[8:]
    half = SRC // 2
    for s in range(half):
        buf[s, :, :] = kv_a[s, :, :]
        buf[half + s, :, :] = kv_b[s, :, :]
    _fill_chunk(buf, kp_ref, vp_ref, 0)
    _accumulate(qa_in, kp_ref, vp_ref, acc_in, acc_ref, 1)
    m_ref[...] = m_in[...]
    good = jnp.max(acc_ref[SUM_ROW : SUM_ROW + 1, :]) < SAFE_SUM

    @pl.when(jnp.logical_not(good))
    def _():
        qa_ref[...] = qa_in[...]
        _redo(qa_ref, m_ref, acc_ref, kp_ref, vp_ref, kvs, buf, sem)

    own_ref[0:56, :] = acc_ref[0:56, 0:NQ]
    own_ref[56:64, :] = m_ref[:, 0:NQ]
    sib_ref[0:56, :] = acc_ref[0:56, NQ:Q2]
    sib_ref[56:64, :] = m_ref[:, NQ:Q2]


def _pair_cost(chunks):
    return _cost(2 * Q2 * CK * 512 * chunks, 4e6, Q2 * CK * chunks)


def _scratch(chunks):
    return [pltpu.VMEM((chunks * CK, KROWS), BF), pltpu.VMEM((ORS, chunks * CK), BF)]


def _first(q_own, q_sib, kv):
    return pl.pallas_call(
        _first_kernel,
        out_shape=(
            jax.ShapeDtypeStruct((KROWS, Q2), BF),
            jax.ShapeDtypeStruct((8, Q2), F32),
            jax.ShapeDtypeStruct((ORS, Q2), F32),
        ),
        in_specs=[VMEM] * 3,
        out_specs=(VMEM,) * 3,
        scratch_shapes=_scratch(1),
        compiler_params=_params(),
        cost_estimate=_pair_cost(1),
        name="attend_own",
    )(q_own, q_sib, kv)


def _next(qa, acc, *kvs):
    n = len(kvs)
    return pl.pallas_call(
        functools.partial(_next_kernel, n),
        out_shape=jax.ShapeDtypeStruct((ORS, Q2), F32),
        in_specs=[VMEM] * (2 + n),
        out_specs=VMEM,
        scratch_shapes=_scratch(n),
        compiler_params=_params(),
        cost_estimate=_pair_cost(n),
        name="attend_ring",
    )(qa, acc, *kvs)


def _last(qa, m, acc, kv_a, kv_b, kvs):
    return pl.pallas_call(
        _last_kernel,
        out_shape=(jax.ShapeDtypeStruct((64, NQ), F32), jax.ShapeDtypeStruct((64, NQ), F32)),
        in_specs=[VMEM] * 5 + [ANY] * 8,
        out_specs=(VMEM, VMEM),
        scratch_shapes=[
            pltpu.VMEM((KROWS, Q2), BF),
            pltpu.VMEM((8, Q2), F32),
            pltpu.VMEM((ORS, Q2), F32),
            *_scratch(1),
            pltpu.VMEM((SRC, 2 * HD, T), BF),
            pltpu.SemaphoreType.DMA,
        ],
        compiler_params=_params(),
        cost_estimate=_pair_cost(1),
        name="attend_last",
    )(qa, m, acc, kv_a, kv_b, *kvs)


def _merge_kernel(a_ref, b_ref, o_ref):
    ma, mb = a_ref[56:57, :], b_ref[56:57, :]
    top = jnp.maximum(ma, mb)
    wa, wb = jnp.exp2(ma - top), jnp.exp2(mb - top)
    total = a_ref[SUM_ROW : SUM_ROW + 1, :] * wa + b_ref[SUM_ROW : SUM_ROW + 1, :] * wb
    out = ((a_ref[0:HD, :] * wa + b_ref[0:HD, :] * wb) / total).astype(BF)
    for s in range(SRC):
        o_ref[s, :, :] = out[:, s * T : (s + 1) * T]


def _merge(a, b):
    return pl.pallas_call(
        _merge_kernel,
        out_shape=jax.ShapeDtypeStruct((SRC, HD, T), BF),
        in_specs=[VMEM, VMEM],
        out_specs=VMEM,
        compiler_params=_params(),
        cost_estimate=_cost(1e6, 2e6),
        name="merge_cores",
    )(a, b)


def _norm_kernel(att_ref, w_ref, gain_ref, shift_ref, o_ref):
    att = att_ref[...].astype(F32).T.astype(BF)
    y = jnp.dot(att, w_ref[...], preferred_element_type=F32)
    center = jnp.mean(y, axis=-1, keepdims=True)
    spread = jnp.mean((y - center) ** 2, axis=-1, keepdims=True)
    o_ref[...] = ((y - center) / jnp.sqrt(spread + 1e-05) * gain_ref[...] + shift_ref[...]).astype(BF)


def _norm(att, w, gain, shift):
    return pl.pallas_call(
        _norm_kernel,
        out_shape=jax.ShapeDtypeStruct((T, D), BF),
        in_specs=[VMEM] * 4,
        out_specs=VMEM,
        compiler_params=_params(),
        cost_estimate=_cost(2 * T * D * D, 2e6),
        name="project_norm",
    )(att, w, gain.reshape(1, D), shift.reshape(1, D))


def _conv_kernel(x_ref, w_ref, b_ref, o_ref, acc_ref):
    step = pl.program_id(0)
    a, b = step // 3, step % 3
    window = x_ref[pl.ds(a, 2), pl.ds(b, 2)].reshape(T, D)
    y = lax.dot_general(
        window, w_ref[...].reshape(3 * COUT, D), (((1,), (1,)), ((), ())), preferred_element_type=F32
    )

    @pl.when(step == 0)
    def _():
        acc_ref[...] = y

    @pl.when(step > 0)
    def _():
        acc_ref[...] += y

    @pl.when(step == 8)
    def _():
        for col in range(4):
            rows = slice(col * 32, (col + 1) * 32)
            first = acc_ref[rows, 0:COUT]
            mid = acc_ref[rows, COUT : 2 * COUT]
            last = acc_ref[rows, 2 * COUT : 3 * COUT]
            first = jnp.concatenate([first[31:32], first[0:31]], axis=0)
            last = jnp.concatenate([last[1:32], last[0:1]], axis=0)
            o_ref[rows, :] = (first + mid + last + b_ref[...]).astype(BF)


def _conv(padded, w, bias):
    return pl.pallas_call(
        _conv_kernel,
        out_shape=jax.ShapeDtypeStruct((T, COUT), BF),
        grid=(9,),
        in_specs=[
            pl.BlockSpec((4, 4, 32, D), lambda i: (0, 0, 0, 0)),
            pl.BlockSpec((3, COUT, D), lambda i: (i, 0, 0)),
            pl.BlockSpec((1, COUT), lambda i: (0, 0)),
        ],
        out_specs=pl.BlockSpec((T, COUT), lambda i: (0, 0)),
        scratch_shapes=[pltpu.VMEM((T, 3 * COUT), F32)],
        compiler_params=_params(),
        cost_estimate=_cost(2 * T * D * COUT * 27, 12e6),
        name="convolution",
    )(padded, w, bias.reshape(1, COUT))


def _linear(y, xh, c, z, xl):
    return (y * 4 + xh * 2 + c) * 16 + z * 2 + xl


PLANES = [
    [_linear(y, xh, c, z, xl) for y in range(4) for xh in range(2) for xl in range(2)]
    for z in range(8)
    for c in range(2)
]


def _plane_swap(x):
    return lax.all_to_all(x, ("gx", "gy"), split_axis=0, concat_axis=0, tiled=True, axis_index_groups=PLANES)


def _core_swap(x):
    return lax.ppermute(x, "gx", [(i, i ^ 1) for i in range(16)])


def _along_z(x, d):
    return lax.ppermute(x, "gy", [(z * 2 + l, ((z + d) % 8) * 2 + l) for z in range(8) for l in range(2)])


def _halo(block):
    up = [(i, (i + 1) % 16) for i in range(16)]
    down = [(i, (i - 1) % 16) for i in range(16)]
    for axis, dim in (("gx", 0), ("gy", 1)):
        size = block.shape[dim]
        low = lax.ppermute(lax.slice_in_dim(block, size - 1, size, axis=dim), axis, up)
        high = lax.ppermute(lax.slice_in_dim(block, 0, 1, axis=dim), axis, down)
        block = jnp.concatenate([low, block, high], axis=dim)
    return block


def shards(tokens, w_qkv, w_out, norm_gain, norm_shift, w_conv, conv_bias):
    packed = _qkv(tokens.reshape(T, D), w_qkv)
    mine = _plane_swap(packed)
    w_taps = jnp.transpose(w_conv, (0, 1, 2, 4, 3)).reshape(27, COUT // 16, D)
    mine, w_taps = lax.optimization_barrier((mine, w_taps))
    taps = lax.all_gather(w_taps, "gx", axis=1, tiled=True)
    q_own, kv = mine[:, :HD], mine[:, HD:]
    up, down = _along_z(kv, 1), _along_z(kv, -1)
    q_sib = _core_swap(q_own)
    qa, m, acc = _first(q_own, q_sib, kv)
    chunks = [kv, up, down]
    for _ in range(2):
        later = (_along_z(up, 1), _along_z(down, -1))
        acc = _next(qa, acc, up, down)
        up, down = later
        chunks += [up, down]
    half = SRC // 2
    far = (_along_z(up[:half], 1), _along_z(down[half:], -1))
    acc = _next(qa, acc, up, down)
    own, sib = _last(qa, m, acc, far[0], far[1], chunks + [jnp.concatenate(far, axis=0)])
    att = _merge(own, _core_swap(sib))
    back = _plane_swap(att).reshape(D, T)
    normed = _norm(back, w_out, norm_gain, norm_shift)
    padded = _halo(normed.reshape(2, 2, 32, D))
    return _conv(padded, taps, conv_bias).reshape(2, 2, 32, COUT)


def solution(mesh):
    return jax.shard_map(
        shards,
        mesh=mesh,
        in_specs=(
            P("gx", "gy", None, None),
            P(),
            P(),
            P(),
            P(),
            P(None, None, None, None, "gx"),
            P(),
        ),
        out_specs=P("gx", "gy", None, None),
        check_vma=False,
    )
```

time: 726 us -> 271 us (0.37)
  matrix products: 293 us -> 0 us
  Pallas kernels: 0 us -> 185 us
  other arithmetic: 140 us -> 0.19 us
  waiting for transfers between devices: 154 us -> 20.4 us
  local copies, waits for them, and re-layouts: 60.1 us -> 4.04 us
  blocking collectives: 48.7 us -> 19.1 us
  starting transfers between devices: 13.7 us -> 25.6 us
    dot_general x61 -> x0, matrix products: 293 us -> none  [the longest x16 147 us: attend_block(): jnp.einsum('qhd,khd->hqk', queries, key_block, preferred_element_type=jnp...]
    pallas_call x0 -> x9, Pallas kernels: none -> 185 us  [the longest x1 118 us: _last(): pl.pallas_call(_last_kernel, out_shape=(jax.ShapeDtypeStruct((64, NQ), F3...]
    reduce_sum x17 -> x0, other arithmetic: 137 us -> none  [the longest x16 137 us: attend_block(): totals = totals * factor + jnp.sum(expons, axis=-1)]
    all_gather x3 -> x1, waiting for transfers between devices: 136 us -> 0.02 us  [shards(): taps = lax.all_gather(w_taps, 'gx', axis=1, tiled=True)]
    another operation x2 -> x0, local copies, waits for them, and re-layouts: 32.5 us -> none  [the longest x1 16.2 us: fold_keys(): keys_piece.reshape(count_k // block_rows, block_rows, heads_here, HEAD_DIM)]
    all_to_all x3 -> x1, blocking collectives: 48.7 us -> 19.1 us  [_plane_swap(): lax.all_to_all(x, ('gx', 'gy'), split_axis=0, concat_axis=0, tiled=True,...]
    ppermute x4 -> x14, starting transfers between devices: 8.43 us -> 22.1 us  [the longest x8 13.1 us: _along_z(): lax.ppermute(x, 'gy', [(z * 2 + l, (z + d) % 8 * 2 + l) for z in range(8)...]
    unnamed x52 -> x14, local copies, waits for them, and re-layouts: 16.7 us -> 3.92 us
  transfers between devices with their start and end apart: 8 -> 16, of which waited for: 6 -> 6; matrix products, arithmetic and copies ran while one was open for 63% -> 0% of each run, Pallas kernels for 0% -> 65%
where the time goes in v1:
time: 271 us; the launch traced here: 268 us
  Pallas kernels  185 us (68%)
  starting transfers between devices  25.6 us (9%)
  waiting for transfers between devices  20.4 us (8%)
  blocking collectives  19.1 us (7%)
  between operations  13.7 us (5%)
  local copies, waits for them, and re-layouts  4.04 us (1%)
    pallas_call x1, Pallas kernels, _last(): pl.pallas_call(_last_kernel, out_shape=(jax.ShapeDtypeStruct((64, NQ), F3...  118 us
    pallas_call x3, Pallas kernels, _next(): pl.pallas_call(functools.partial(_next_kernel, n), out_shape=jax.ShapeDty...  45.6 us
    all_to_all x1, blocking collectives, _plane_swap(): lax.all_to_all(x, ('gx', 'gy'), split_axis=0, concat_axis=0, tiled=True,...  19.1 us
    ppermute x8, starting transfers between devices, _along_z(): lax.ppermute(x, 'gy', [(z * 2 + l, (z + d) % 8 * 2 + l) for z in range(8)...  13.1 us
    pallas_call x1, Pallas kernels, _conv(): pl.pallas_call(_conv_kernel, out_shape=jax.ShapeDtypeStruct((T, COUT), BF...  10 us
    pallas_call x1, Pallas kernels, _first(): pl.pallas_call(_first_kernel, out_shape=(jax.ShapeDtypeStruct((KROWS, Q2)...  9.27 us
    all_to_all x1, waiting for transfers between devices, _plane_swap(): lax.all_to_all(x, ('gx', 'gy'), split_axis=0, concat_axis=0, tiled=True,...  8.48 us
    ppermute x2, starting transfers between devices, _halo(): high = lax.ppermute(lax.slice_in_dim(block, 0, 1, axis=dim), axis, down)  8.08 us
  transfers between devices with their start and end apart: 16, of which 6 were waited for; matrix products, arithmetic and copies ran while one was open for 0% of the time, Pallas kernels for 65%

profile of v1, /device:TPU:32, one launch (start us, length us, event | category | flops | bytes accessed | tf_op | source)
XLA Modules:
  0.0 268.1 jit_solution(15941811894376829486)
XLA Ops:
  6.5 2.0 copy-done
  8.5 0.9 copy-done.2
  9.5 0.7 qkv_projection.1
  10.2 19.1 %all_to_all.10 = bf16[16,144,128]{2,1,0:T(8,128)(2,1)S(1)} all-to-all(bf16[16,144,128]{2,1,0:T(8,128)(2,1)S(1)} %qkv_projection.1), channel_id=1, replica_groups={{0,1,32,33,64,65,96,97,128,129,160,161,192,193,224,225},{16,17,48,49,80..., dimensions={0} | all-to-all | bytes 1179648 | tf_op jit(solution)/shard_map/all_to_all | solution.py:362
  29.5 2.0 collective-permute-start.1
  31.5 0.1 collective-permute-start.2
  31.6 9.3 %attend_own.1 = (bf16[128,4096]{1,0:T(8,128)(2,1)S(1)}, f32[8,4096]{1,0:T(8,128)S(1)}, f32[64,4096]{1,0:T(8,128)S(1)}) custom-call(bf16[16,48,128]{2,1,0:T(8,128)(2,1)S(1)} %slice.30.q_own, bf16[16,48,128]{2,1,0:T(8,128)(2,1)S(1)} %collective-permute-done.q_sib, bf16[16,96,128]{2,1,0:T(8,128)(2,1)S(1)} %slice.31.kv_ref.refs_0_), custom_call_target="tpu_custom_call" | custom-call | flops 8589934592 | bytes 4000000 | tf_op jit(solution)/shard_map/attend_own/pallas_call | solution.py:212
  40.9 0.2 collective-permute-done.1.refs_0_.refs_1_
  41.1 1.9 collective-permute-start.3
  43.0 2.3 collective-permute-start.4
  45.3 15.2 %attend_ring.3.acc_in = f32[64,4096]{1,0:T(8,128)S(1)} custom-call(bf16[128,4096]{1,0:T(8,128)(2,1)S(1)} %get-tuple-element.13.qa_ref.qa_in, f32[64,4096]{1,0:T(8,128)S(1)} %get-tuple-element.15.acc_in, bf16[16,96,128]{2,1,0:T(8,128)(2,1)S(1)} %collective-permute-done.1.refs_0_.refs_1_, bf16[16,96,128]{2,1,0:T(8,128)(2,1)S(1)} %collective-permute-done.2.refs_1_.refs_2_), custom_call_target="tpu_custom_call" | custom-call | flops 17179869184 | bytes 4000000 | tf_op jit(solution)/shard_map/attend_ring/pallas_call | solution.py:230
  60.5 0.8 collective-permute-start.5
  61.3 2.8 %collective-permute-start.6 = (bf16[16,96,128]{2,1,0:T(8,128)(2,1)S(1)}, bf16[16,96,128]{2,1,0:T(8,128)(2,1)S(1)}, u32[]{:S(2)}, u32[]{:S(2)}) collective-permute-start(bf16[16,96,128]{2,1,0:T(8,128)(2,1)S(1)} %collective-permute-done.4.refs_1_.refs_4_), channel_id=1, source_target_pairs={{0,14},{1,15},{2,0},{3,1},{4,2},{5,3},{6,4},{7,5},{8,6},{9,7},{10,... | collective-permute-start | bytes 1179656 | tf_op jit(solution)/shard_map/ppermute | solution.py:370
  64.1 15.2 %attend_ring.4.acc_in = f32[64,4096]{1,0:T(8,128)S(1)} custom-call(bf16[128,4096]{1,0:T(8,128)(2,1)S(1)} %get-tuple-element.13.qa_ref.qa_in, f32[64,4096]{1,0:T(8,128)S(1)} %attend_ring.3.acc_in, bf16[16,96,128]{2,1,0:T(8,128)(2,1)S(1)} %collective-permute-done.3.refs_0_.refs_3_, bf16[16,96,128]{2,1,0:T(8,128)(2,1)S(1)} %collective-permute-done.4.refs_1_.refs_4_), custom_call_target="tpu_custom_call" | custom-call | flops 17179869184 | bytes 4000000 | tf_op jit(solution)/shard_map/attend_ring/pallas_call | solution.py:230
  79.4 0.5 collective-permute-start.7
  79.9 2.6 collective-permute-start.8
  82.5 15.2 %attend_ring.5.acc_in = f32[64,4096]{1,0:T(8,128)S(1)} custom-call(bf16[128,4096]{1,0:T(8,128)(2,1)S(1)} %get-tuple-element.13.qa_ref.qa_in, f32[64,4096]{1,0:T(8,128)S(1)} %attend_ring.4.acc_in, bf16[16,96,128]{2,1,0:T(8,128)(2,1)S(1)} %collective-permute-done.5.refs_0_.refs_5_, bf16[16,96,128]{2,1,0:T(8,128)(2,1)S(1)} %collective-permute-done.6.refs_1_.refs_6_), custom_call_target="tpu_custom_call" | custom-call | flops 17179869184 | bytes 4000000 | tf_op jit(solution)/shard_map/attend_ring/pallas_call | solution.py:230
  97.8 1.0 copy-done.4
  98.8 118.2 %attend_last.1 = (f32[64,2048]{1,0:T(8,128)S(1)}, f32[64,2048]{1,0:T(8,128)S(1)}) custom-call(bf16[128,4096]{1,0:T(8,128)(2,1)S(1)} %get-tuple-element.13.qa_ref.qa_in, f32[8,4096]{1,0:T(8,128)S(1)} %get-tuple-element.14.m_in, f32[64,4096]{1,0:T(8,128)} %copy-done.4, bf16[8,96,128]{2,1,0:T(8,128)(2,1)S(1)} %collective-permute-done.7.kv_a, ...), custom_call_target="tpu_custom_call" | custom-call | flops 8589934592 | bytes 4000000 | tf_op jit(solution)/shard_map/attend_last/pallas_call | solution.py:243
  217.1 1.9 collective-permute-done.9.b_ref
  219.0 0.8 merge_cores.1
  219.8 3.5 %all-to-all-start.1 = ((bf16[16,48,128]{2,1,0:T(8,128)(2,1)}), bf16[16,48,128]{2,1,0:T(8,128)(2,1)S(1)}, u32[]{:S(2)}, u32[]{:S(2)}) async-start(bf16[16,48,128]{2,1,0:T(8,128)(2,1)} %merge_cores.1), calls=%async_computation.1 | async-start | bytes 393216 | tf_op jit(solution)/shard_map/all_to_all | solution.py:362
  223.4 8.5 %all-to-all-done.1 = bf16[16,48,128]{2,1,0:T(8,128)(2,1)S(1)} async-done(((bf16[16,48,128]{2,1,0:T(8,128)(2,1)}), bf16[16,48,128]{2,1,0:T(8,128)(2,1)S(1)}, u32[]{:S(2)}, u32[]{:S(2)}) %all-to-all-start.1) | async-done | bytes 196640 | tf_op jit(solution)/shard_map/all_to_all | solution.py:362
  231.8 0.6 project_norm.1
  232.6 5.3 %collective-permute-start.11 = (bf16[1,2,32,768]{3,2,1,0:T(8,128)(2,1)S(1)}, bf16[1,2,32,768]{3,2,1,0:T(8,128)(2,1)S(1)}, u32[]{:S(2)}, u32[]{:S(2)}) collective-permute-start(bf16[1,2,32,768]{3,2,1,0:T(8,128)(2,1)S(1)} %bitcast.16), channel_id=1, source_target_pairs={{0,240},{16,0},{32,16},{48,32},{64,48},{80,64},{96,80},{112,96},{1... | collective-permute-start | bytes 294920 | tf_op jit(solution)/shard_map/ppermute | solution.py:379
  237.9 3.2 %collective-permute-done.10 = bf16[1,2,32,768]{3,2,1,0:T(8,128)(2,1)S(1)} collective-permute-done((bf16[1,2,32,768]{3,2,1,0:T(8,128)(2,1)S(1)}, bf16[1,2,32,768]{3,2,1,0:T(8,128)(2,1)S(1)}, u32[]{:S(2)}, u32[]{:S(2)}) %collective-permute-start.10) | collective-permute-done | bytes 98336 | tf_op jit(solution)/shard_map/ppermute | solution.py:378
  241.2 0.6 collective-permute-start.12
  241.8 2.7 %collective-permute-start.13 = (bf16[4,1,32,768]{3,2,1,0:T(8,128)(2,1)S(1)}, bf16[4,1,32,768]{3,2,1,0:T(8,128)(2,1)S(1)}, u32[]{:S(2)}, u32[]{:S(2)}) collective-permute-start(bf16[4,1,32,768]{3,2,1,0:T(8,128)(2,1)S(1)} %get-tuple-element.20), channel_id=1, source_target_pairs={{0,15},{1,0},{2,1},{3,2},{4,3},{5,4},{6,5},{7,6},{8,7},{9,8},{10,9... | collective-permute-start | bytes 589832 | tf_op jit(solution)/shard_map/ppermute | solution.py:379
  244.5 4.4 %collective-permute-done.12 = bf16[4,1,32,768]{3,2,1,0:T(8,128)(2,1)S(1)} collective-permute-done((bf16[4,1,32,768]{3,2,1,0:T(8,128)(2,1)S(1)}, bf16[4,1,32,768]{3,2,1,0:T(8,128)(2,1)S(1)}, u32[]{:S(2)}, u32[]{:S(2)}) %collective-permute-start.12) | collective-permute-done | bytes 196640 | tf_op jit(solution)/shard_map/ppermute | solution.py:378
  249.0 2.1 collective-permute-done.13
  251.1 0.1 pad_maximum_fusion.x_ref
  251.2 10.0 %convolution.1 = bf16[128,256]{1,0:T(8,128)(2,1)} custom-call(bf16[4,4,32,768]{3,2,1,0:T(8,128)(2,1)S(1)} %pad_maximum_fusion.x_ref, bf16[27,256,768]{2,1,0:T(8,128)(2,1)} %all-gather.2.cloned.1.call-done.w_ref, f32[1,256]{1,0:T(1,128)S(1)} %bitcast.14), custom_call_target="tpu_custom_call" | custom-call | flops 1358954496 | bytes 12000000 | tf_op jit(solution)/shard_map/convolution/pallas_call | solution.py:333
  (36 shorter events, 0.6 us)
Async XLA Ops:
  6.5 244.7 %all-gather.2.cloned.1.call-start = ((), (), s32[]{:S(2)}) async-start(), calls=%async_computation.2 | async-start | bytes 11280384 | tf_op jit(solution)/shard_map/all_gather | solution.py:389
  6.5 2.0 copy-start
  8.5 0.9 copy-start.2
  29.3 2.2 collective-permute-start
  29.5 11.6 %collective-permute-start.1 = (bf16[16,96,128]{2,1,0:T(8,128)(2,1)S(1)}, bf16[16,96,128]{2,1,0:T(8,128)(2,1)S(1)}, u32[]{:S(2)}, u32[]{:S(2)}) collective-permute-start(bf16[16,96,128]{2,1,0:T(8,128)(2,1)S(1)} %slice.31.kv_ref.refs_0_), channel_id=1, source_target_pairs={{0,2},{1,3},{2,4},{3,5},{4,6},{5,7},{6,8},{7,9},{8,10},{9,11},{10,... | collective-permute-start | bytes 1179656 | tf_op jit(solution)/shard_map/ppermute | solution.py:370
  31.5 11.5 %collective-permute-start.2 = (bf16[16,96,128]{2,1,0:T(8,128)(2,1)S(1)}, bf16[16,96,128]{2,1,0:T(8,128)(2,1)S(1)}, u32[]{:S(2)}, u32[]{:S(2)}) collective-permute-start(bf16[16,96,128]{2,1,0:T(8,128)(2,1)S(1)} %slice.31.kv_ref.refs_0_), channel_id=1, source_target_pairs={{0,14},{1,15},{2,0},{3,1},{4,2},{5,3},{6,4},{7,5},{8,6},{9,7},{10,... | collective-permute-start | bytes 1179656 | tf_op jit(solution)/shard_map/ppermute | solution.py:370
  41.1 19.5 %collective-permute-start.3 = (bf16[16,96,128]{2,1,0:T(8,128)(2,1)S(1)}, bf16[16,96,128]{2,1,0:T(8,128)(2,1)S(1)}, u32[]{:S(2)}, u32[]{:S(2)}) collective-permute-start(bf16[16,96,128]{2,1,0:T(8,128)(2,1)S(1)} %collective-permute-done.1.refs_0_.refs_1_), channel_id=1, source_target_pairs={{0,2},{1,3},{2,4},{3,5},{4,6},{5,7},{6,8},{7,9},{8,10},{9,11},{10,... | collective-permute-start | bytes 1179656 | tf_op jit(solution)/shard_map/ppermute | solution.py:370
  43.0 18.3 %collective-permute-start.4 = (bf16[16,96,128]{2,1,0:T(8,128)(2,1)S(1)}, bf16[16,96,128]{2,1,0:T(8,128)(2,1)S(1)}, u32[]{:S(2)}, u32[]{:S(2)}) collective-permute-start(bf16[16,96,128]{2,1,0:T(8,128)(2,1)S(1)} %collective-permute-done.2.refs_1_.refs_2_), channel_id=1, source_target_pairs={{0,14},{1,15},{2,0},{3,1},{4,2},{5,3},{6,4},{7,5},{8,6},{9,7},{10,... | collective-permute-start | bytes 1179656 | tf_op jit(solution)/shard_map/ppermute | solution.py:370
  60.5 18.8 %collective-permute-start.5 = (bf16[16,96,128]{2,1,0:T(8,128)(2,1)S(1)}, bf16[16,96,128]{2,1,0:T(8,128)(2,1)S(1)}, u32[]{:S(2)}, u32[]{:S(2)}) collective-permute-start(bf16[16,96,128]{2,1,0:T(8,128)(2,1)S(1)} %collective-permute-done.3.refs_0_.refs_3_), channel_id=1, source_target_pairs={{0,2},{1,3},{2,4},{3,5},{4,6},{5,7},{6,8},{7,9},{8,10},{9,11},{10,... | collective-permute-start | bytes 1179656 | tf_op jit(solution)/shard_map/ppermute | solution.py:370
  61.3 18.6 %collective-permute-start.6 = (bf16[16,96,128]{2,1,0:T(8,128)(2,1)S(1)}, bf16[16,96,128]{2,1,0:T(8,128)(2,1)S(1)}, u32[]{:S(2)}, u32[]{:S(2)}) collective-permute-start(bf16[16,96,128]{2,1,0:T(8,128)(2,1)S(1)} %collective-permute-done.4.refs_1_.refs_4_), channel_id=1, source_target_pairs={{0,14},{1,15},{2,0},{3,1},{4,2},{5,3},{6,4},{7,5},{8,6},{9,7},{10,... | collective-permute-start | bytes 1179656 | tf_op jit(solution)/shard_map/ppermute | solution.py:370
  79.4 19.4 %collective-permute-start.7 = (bf16[8,96,128]{2,1,0:T(8,128)(2,1)S(1)}, bf16[8,96,128]{2,1,0:T(8,128)(2,1)S(1)}, u32[]{:S(2)}, u32[]{:S(2)}) collective-permute-start(bf16[8,96,128]{2,1,0:T(8,128)(2,1)S(1)} %slice.40), channel_id=1, source_target_pairs={{0,2},{1,3},{2,4},{3,5},{4,6},{5,7},{6,8},{7,9},{8,10},{9,11},{10,... | collective-permute-start | bytes 589832 | tf_op jit(solution)/shard_map/ppermute | solution.py:370
  79.9 18.8 %collective-permute-start.8 = (bf16[8,96,128]{2,1,0:T(8,128)(2,1)S(1)}, bf16[8,96,128]{2,1,0:T(8,128)(2,1)S(1)}, u32[]{:S(2)}, u32[]{:S(2)}) collective-permute-start(bf16[8,96,128]{2,1,0:T(8,128)(2,1)S(1)} %slice.41), channel_id=1, source_target_pairs={{0,14},{1,15},{2,0},{3,1},{4,2},{5,3},{6,4},{7,5},{8,6},{9,7},{10,... | collective-permute-start | bytes 589832 | tf_op jit(solution)/shard_map/ppermute | solution.py:370
  97.8 1.0 copy-start.4
  98.8 124.5 %copy-start.5 = (f32[768]{0:T(1024)S(1)}, f32[768]{0:T(1024)}, u32[]{:S(2)}) copy-start(f32[768]{0:T(1024)} %param.10) | copy-start | bytes 9220
  98.8 124.6 %copy-start.6 = (f32[768]{0:T(1024)S(1)}, f32[768]{0:T(1024)}, u32[]{:S(2)}) copy-start(f32[768]{0:T(1024)} %param.11) | copy-start | bytes 9220
  98.8 133.0 %copy-start.1 = (bf16[768,768]{1,0:T(8,128)(2,1)S(1)}, bf16[768,768]{1,0:T(8,128)(2,1)}, u32[]{:S(2)}) copy-start(bf16[768,768]{1,0:T(8,128)(2,1)} %w_ref.3) | copy-start | bytes 3538948
  217.0 34.2 %copy-start.3 = (f32[256]{0:T(256)S(1)}, f32[256]{0:T(256)}, u32[]{:S(2)}) copy-start(f32[256]{0:T(256)} %param.13) | copy-start | bytes 3076
  217.0 2.0 collective-permute-start.9
  219.8 12.1 %all-to-all-start.1 = ((bf16[16,48,128]{2,1,0:T(8,128)(2,1)}), bf16[16,48,128]{2,1,0:T(8,128)(2,1)S(1)}, u32[]{:S(2)}, u32[]{:S(2)}) async-start(bf16[16,48,128]{2,1,0:T(8,128)(2,1)} %merge_cores.1), calls=%async_computation.1 | async-start | bytes 393216 | tf_op jit(solution)/shard_map/all_to_all | solution.py:362
  232.5 8.6 %collective-permute-start.10 = (bf16[1,2,32,768]{3,2,1,0:T(8,128)(2,1)S(1)}, bf16[1,2,32,768]{3,2,1,0:T(8,128)(2,1)S(1)}, u32[]{:S(2)}, u32[]{:S(2)}) collective-permute-start(bf16[1,2,32,768]{3,2,1,0:T(8,128)(2,1)S(1)} %bitcast.17), channel_id=1, source_target_pairs={{0,16},{16,32},{32,48},{48,64},{64,80},{80,96},{96,112},{112,128},... | collective-permute-start | bytes 294920 | tf_op jit(solution)/shard_map/ppermute | solution.py:378
  232.6 8.5 %collective-permute-start.11 = (bf16[1,2,32,768]{3,2,1,0:T(8,128)(2,1)S(1)}, bf16[1,2,32,768]{3,2,1,0:T(8,128)(2,1)S(1)}, u32[]{:S(2)}, u32[]{:S(2)}) collective-permute-start(bf16[1,2,32,768]{3,2,1,0:T(8,128)(2,1)S(1)} %bitcast.16), channel_id=1, source_target_pairs={{0,240},{16,0},{32,16},{48,32},{64,48},{80,64},{96,80},{112,96},{1... | collective-permute-start | bytes 294920 | tf_op jit(solution)/shard_map/ppermute | solution.py:379
  241.2 7.8 %collective-permute-start.12 = (bf16[4,1,32,768]{3,2,1,0:T(8,128)(2,1)S(1)}, bf16[4,1,32,768]{3,2,1,0:T(8,128)(2,1)S(1)}, u32[]{:S(2)}, u32[]{:S(2)}) collective-permute-start(bf16[4,1,32,768]{3,2,1,0:T(8,128)(2,1)S(1)} %get-tuple-element.19), channel_id=1, source_target_pairs={{0,1},{1,2},{2,3},{3,4},{4,5},{5,6},{6,7},{7,8},{8,9},{9,10},{10,1... | collective-permute-start | bytes 589832 | tf_op jit(solution)/shard_map/ppermute | solution.py:378
  241.8 9.3 %collective-permute-start.13 = (bf16[4,1,32,768]{3,2,1,0:T(8,128)(2,1)S(1)}, bf16[4,1,32,768]{3,2,1,0:T(8,128)(2,1)S(1)}, u32[]{:S(2)}, u32[]{:S(2)}) collective-permute-start(bf16[4,1,32,768]{3,2,1,0:T(8,128)(2,1)S(1)} %get-tuple-element.20), channel_id=1, source_target_pairs={{0,15},{1,0},{2,1},{3,2},{4,3},{5,4},{6,5},{7,6},{8,7},{9,8},{10,9... | collective-permute-start | bytes 589832 | tf_op jit(solution)/shard_map/ppermute | solution.py:379
Sparse Core Ops, SparseCore 0:
  29.4 86.3 all-gather.1
